TPU v7x, 32 devices: a whole 2x2x4 slice. The times are simulated.
32 devices in a mesh: blk: 8 (over y, x, core), head: 4 (over z).
Axes of the slice: x: 2, y: 2, z: 4, core: 2. Of those that a mesh axis runs over, the one named last changes fastest.
Arguments:
- queries: bfloat16 [4096, 2048], P(('blk', 'head')), may hold values from -6 to 6
- key_rows: bfloat16 [4096, 2048], P(('blk', 'head')), may hold values from -6 to 6
- value_rows: bfloat16 [4096, 2048], P(('blk', 'head')), may hold values from -6 to 6
- w_out: bfloat16 [2048, 2048], P('head'), may hold values from -0.125 to 0.125
- first_key: int32 [4096], P('blk'), may hold values from 0 to 4093, as said below
Outputs:
- mixed: bfloat16 [4096, 2048], P(('blk', 'head'))
Inputs may be any that keep to these rules, and one draw needn't show every extreme that they name: first_key[i] <= max(i - 1, 0) and first_key[i] >= i - 512; the last bin of each aligned block of 512 bins has first_key exactly i - 512 where that is not negative; the next-to-last bin of the sequence has first_key exactly 4093.
All inputs are finite; a program needn't handle non-finite values.
Results may differ from a plain program's by a relative error of at most 0.0055.
Values may be sent and summed in bfloat16 or wider, within the bound.
A program may use at most 64 MiB of HBM per device.

v0:
```python
import jax
import jax.numpy as jnp
from jax import lax
from jax.sharding import PartitionSpec as P

HEAD_DIM = 64


def from_behind(x, axis, by):
    devices = lax.axis_size(axis)
    pairs = [(i, i + by) for i in range(devices) if 0 <= i + by < devices]
    return lax.ppermute(x, axis, pairs)


def attend(query_tile, key_tile, value_tile, lowest, query_pos, key_pos):
    scores = lax.dot_general(
        query_tile, key_tile, (((1,), (1,)), ((), ())), preferred_element_type=jnp.float32
    )
    scores = scores * HEAD_DIM ** (-0.5)
    allowed = (key_pos[None, :] >= lowest[:, None]) & (key_pos[None, :] <= query_pos[:, None])
    scores = jnp.where(allowed, scores, -jnp.inf)
    largest = jnp.max(scores, axis=1, keepdims=True)
    powers = jnp.exp(scores - largest)
    totals = jnp.sum(powers, axis=1, keepdims=True)
    weights = powers.astype(jnp.bfloat16)
    context = jnp.dot(weights, value_tile, preferred_element_type=jnp.float32) / totals
    return context.astype(jnp.bfloat16)


def on_device(queries, key_rows, value_rows, w_out, first_key):
    place = lax.axis_index("blk")
    query_h, key_h, value_h = (
        lax.all_to_all(queries, "head", split_axis=1, concat_axis=0, tiled=True),
        lax.all_to_all(key_rows, "head", split_axis=1, concat_axis=0, tiled=True),
        lax.all_to_all(value_rows, "head", split_axis=1, concat_axis=0, tiled=True),
    )
    earlier = from_behind(jnp.stack((key_h, value_h)), "blk", 1)
    key_prev = earlier[0]
    value_prev = earlier[1]
    span_rows = query_h.shape[0]
    width = query_h.shape[1]
    local_heads = width // HEAD_DIM
    key_all = jnp.concatenate([key_prev, key_h], axis=0)
    value_all = jnp.concatenate([value_prev, value_h], axis=0)
    start = place * span_rows
    query_span = min(512, span_rows)
    spans = span_rows // query_span
    key_count = span_rows + query_span

    def one_tile(item):
        span_id = item // local_heads
        head_id = item % local_heads
        row_start = span_id * query_span
        column = head_id * HEAD_DIM
        query_tile = lax.dynamic_slice(query_h, (row_start, column), (query_span, HEAD_DIM))
        key_tile = lax.dynamic_slice(key_all, (row_start, column), (key_count, HEAD_DIM))
        value_tile = lax.dynamic_slice(value_all, (row_start, column), (key_count, HEAD_DIM))
        lowest = lax.dynamic_slice_in_dim(first_key, row_start, query_span)
        query_pos = start + row_start + jnp.arange(query_span, dtype=jnp.int32)
        key_pos = start - span_rows + row_start + jnp.arange(key_count, dtype=jnp.int32)
        return attend(query_tile, key_tile, value_tile, lowest, query_pos, key_pos)

    tiles = lax.map(one_tile, jnp.arange(spans * local_heads, dtype=jnp.int32))
    context = (
        tiles.reshape(spans, local_heads, query_span, HEAD_DIM)
        .transpose(0, 2, 1, 3)
        .reshape(span_rows, width)
    )
    regrouped = lax.all_to_all(context, "head", split_axis=0, concat_axis=1, tiled=True)
    summed = jnp.dot(
        regrouped,
        lax.all_gather(w_out, "head", axis=0, tiled=True),
        preferred_element_type=jnp.float32,
    )
    return summed.astype(jnp.bfloat16)


def solution(mesh):
    placed = (
        P(("blk", "head"), None),
        P(("blk", "head"), None),
        P(("blk", "head"), None),
        P("head", None),
        P("blk"),
    )
    return jax.shard_map(
        on_device, mesh=mesh, in_specs=placed, out_specs=P(("blk", "head"), None), check_vma=False
    )
```

profile of v0, /device:TPU:0, one launch (start us, length us, event | category | flops | bytes accessed | tf_op | source)
XLA Modules:
  0.0 210.7 jit_solution(14317576022515698305)
XLA Ops:
  8.4 6.3 %all-to-all-start.1 = ((bf16[128,4,512]{2,0,1:T(8,128)(2,1)}), bf16[128,4,512]{2,0,1:T(8,128)(2,1)S(1)}, u32[]{:S(2)}, u32[]{:S(2)}) async-start(bf16[128,4,512]{2,0,1:T(8,128)(2,1)} %bitcast.44), calls=%async_computation.1 | async-start | bytes 1048576 | tf_op jit(solution)/shard_map/all_to_all | solution.py:34
  14.8 23.0 %all-to-all-done.1 = bf16[128,4,512]{2,0,1:T(8,128)(2,1)S(1)} async-done(((bf16[128,4,512]{2,0,1:T(8,128)(2,1)}), bf16[128,4,512]{2,0,1:T(8,128)(2,1)S(1)}, u32[]{:S(2)}, u32[]{:S(2)}) %all-to-all-start.1) | async-done | bytes 524320 | tf_op jit(solution)/shard_map/all_to_all | solution.py:34
  37.8 39.2 %all_to_all.76 = bf16[128,4,512]{2,0,1:T(8,128)(2,1)S(1)} all-to-all(bf16[128,4,512]{2,0,1:T(8,128)(2,1)S(1)} %bitcast.55), channel_id=1, replica_groups=mesh['blk'=8,'head'=4] {'head'}, dimensions={1} | all-to-all | bytes 1048576 | tf_op jit(solution)/shard_map/all_to_all | solution.py:35
  77.1 1.4 collective-permute-start
  78.5 1.9 copy.28
  80.4 4.2 %all-to-all-start = ((bf16[128,4,512]{2,0,1:T(8,128)(2,1)}), bf16[128,4,512]{2,0,1:T(8,128)(2,1)}, u32[]{:S(2)}, u32[]{:S(2)}) async-start(bf16[128,4,512]{2,0,1:T(8,128)(2,1)} %bitcast.45), calls=%async_computation | async-start | bytes 1048576 | tf_op jit(solution)/shard_map/all_to_all | solution.py:33
  84.8 26.6 %all-to-all-done = bf16[128,4,512]{2,0,1:T(8,128)(2,1)} async-done(((bf16[128,4,512]{2,0,1:T(8,128)(2,1)}), bf16[128,4,512]{2,0,1:T(8,128)(2,1)}, u32[]{:S(2)}, u32[]{:S(2)}) %all-to-all-start) | async-done | bytes 524320 | tf_op jit(solution)/shard_map/all_to_all | solution.py:33
  111.4 49.9 %while.12 = (s32[]{:T(128)}, bf16[8,512,64]{1,2,0:T(8,128)(2,1)}, s32[8]{0:T(128)S(1)}, s32[]{:T(128)}, s32[512]{0:T(512)S(1)}, /*index=5*/s32[]{:T(128)}, bf16[...) while((s32[]{:T(128)}, bf16[8,512,64]{1,2,0:T(8,128)(2,1)}, ...), condition=%wide.region_3.4_spmd, body=%wide.region_0.3_spmd.sunk | while | flops 139526688 | bytes 7038914 | solution.py:63
  114.2 1.7 fusion.22
  116.4 1.3 fusion.24
  120.5 1.7 fusion.22
  126.7 1.6 fusion.22
  132.9 1.7 fusion.22
  135.1 1.3 fusion.24
  139.2 1.7 fusion.22
  141.3 1.3 fusion.24
  145.4 1.7 fusion.22
  147.6 1.3 fusion.24
  151.7 1.7 fusion.22
  153.8 1.3 fusion.24
  157.9 1.7 fusion.22
  162.6 29.6 %all_to_all.77 = bf16[4,128,512]{1,2,0:T(8,128)(2,1)S(1)} all-to-all(bf16[4,128,512]{1,2,0:T(8,128)(2,1)S(1)} %copy.19), channel_id=1, replica_groups=mesh['blk'=8,'head'=4] {'head'}, dimensions={0} | all-to-all | bytes 1048576 | tf_op jit(solution)/shard_map/all_to_all | solution.py:69
  192.2 6.1 %all-gather.2.cloned.1.call-done = bf16[2048,2048]{1,0:T(8,128)(2,1)} async-done(((bf16[512,2048]{1,0:T(8,128)(2,1)}), bf16[2048,2048]{1,0:T(8,128)(2,1)}) %all-gather.2.cloned.1.call-update) | async-done | bytes 8388624 | tf_op jit(solution)/shard_map/all_gather | solution.py:72
  198.4 5.5 %convolution_convert_fusion = bf16[128,2048]{1,0:T(8,128)(2,1)} fusion(bf16[128,2048]{0,1:T(8,128)(2,1)S(1)} %bitcast.54, bf16[2048,2048]{1,0:T(8,128)(2,1)} %all-gather.2.cloned.1.call-done), kind=kOutput, calls=%fused_computation.16 | convolution fusion | flops 1074003968 | bytes 9437184 | tf_op jit(solution)/shard_map/dot_general | solution.py:70
  (53 shorter events, 15.8 us)
Async XLA Ops:
  6.5 1.0 copy-start
  6.5 8.2 %copy-start.1 = (bf16[128,2048]{1,0:T(8,128)(2,1)S(1)}, bf16[128,2048]{1,0:T(8,128)(2,1)}, u32[]{:S(2)}) copy-start(bf16[128,2048]{1,0:T(8,128)(2,1)} %param.9) | copy-start | bytes 1572868
  6.5 191.8 %all-gather.2.cloned.1.call-start = ((), (), s32[]{:S(2)}) async-start(), calls=%async_computation.4 | async-start | bytes 10485760 | tf_op jit(solution)/shard_map/all_gather | solution.py:72
  8.4 29.3 %all-to-all-start.1 = ((bf16[128,4,512]{2,0,1:T(8,128)(2,1)}), bf16[128,4,512]{2,0,1:T(8,128)(2,1)S(1)}, u32[]{:S(2)}, u32[]{:S(2)}) async-start(bf16[128,4,512]{2,0,1:T(8,128)(2,1)} %bitcast.44), calls=%async_computation.1 | async-start | bytes 1048576 | tf_op jit(solution)/shard_map/all_to_all | solution.py:34
  77.1 7.5 %collective-permute-start = (bf16[2,512,512]{2,1,0:T(8,128)(2,1)S(1)}, bf16[2,512,512]{2,1,0:T(8,128)(2,1)S(1)}, u32[]{:S(2)}, u32[]{:S(2)}) collective-permute-start(bf16[2,512,512]{2,1,0:T(8,128)(2,1)S(1)} %pad_maximum_fusion), channel_id=1, source_target_pairs={{0,4},{4,8},{8,12},{12,16},{16,20},{20,24},{24,28},{1,5},{5,9},{9,... | collective-permute-start | bytes 3145736 | tf_op jit(solution)/shard_map/ppermute | solution.py:12
  80.4 31.0 %all-to-all-start = ((bf16[128,4,512]{2,0,1:T(8,128)(2,1)}), bf16[128,4,512]{2,0,1:T(8,128)(2,1)}, u32[]{:S(2)}, u32[]{:S(2)}) async-start(bf16[128,4,512]{2,0,1:T(8,128)(2,1)} %bitcast.45), calls=%async_computation | async-start | bytes 1048576 | tf_op jit(solution)/shard_map/all_to_all | solution.py:33
  84.7 26.7 %copy-start.2 = (s32[512]{0:T(512)S(1)}, s32[512]{0:T(512)}, u32[]{:S(2)}) copy-start(s32[512]{0:T(512)} %param.11) | copy-start | bytes 6148
Sparse Core Ops, SparseCore 0:
  8.9 189.3 all-gather.1
where the time goes:
time: 212 us; the launch traced here: 211 us
  blocking collectives  68.9 us (33%)
  waiting for transfers between devices  56.4 us (27%)
  matrix products  28.8 us (14%)
  loops' own time  18 us (8%)
  between operations  13.5 us (6%)
  starting transfers between devices  11.8 us (6%)
  local copies, waits for them, and re-layouts  8.85 us (4%)
  other arithmetic  4.42 us (2%)
    all_to_all x1, blocking collectives, on_device(): lax.all_to_all(value_rows, 'head', split_axis=1, concat_axis=0, tiled=True)  39.2 us
    all_to_all x1, blocking collectives, on_device(): lax.all_to_all(context, 'head', split_axis=0, concat_axis=1, tiled=True)  29.6 us
    all_to_all x1, waiting for transfers between devices, on_device(): lax.all_to_all(queries, 'head', split_axis=1, concat_axis=0, tiled=True)  26.6 us
    all_to_all x1, waiting for transfers between devices, on_device(): lax.all_to_all(key_rows, 'head', split_axis=1, concat_axis=0, tiled=True)  23 us
    another operation x1, loops' own time, on_device(): tiles = lax.map(one_tile, jnp.arange(spans * local_heads, dtype=jnp.int32))  18 us
    dot_general x8, matrix products, attend(): lax.dot_general(query_tile, key_tile, (((1,), (1,)), ((), ())), preferred...  13.2 us
    dot_general x8, matrix products, attend(): jnp.dot(weights, value_tile, preferred_element_type=jnp.float32) / totals  10.1 us
    all_to_all x1, starting transfers between devices, on_device(): lax.all_to_all(key_rows, 'head', split_axis=1, concat_axis=0, tiled=True)  6.32 us
  transfers between devices with their start and end apart: 4, of which 3 were waited for; matrix products, arithmetic and copies ran while one was open for 17% of the time, Pallas kernels for 0%

commit v1 on v0

v1 whole, which is shorter than its diff:
```python
import functools
import math

import jax
import jax.numpy as jnp
from jax import lax
from jax.experimental import pallas as pl
from jax.experimental.pallas import tpu as pltpu
from jax.sharding import PartitionSpec as P

HEAD_DIM = 64
PAIR = 2 * HEAD_DIM
MESH = pl.DeviceIdType.MESH
SCALE = HEAD_DIM ** (-0.5) * math.log2(math.e)


def kernel(
    n_blk, n_head, q_in, k_in, v_in, w_in, low_ref, out_ref,
    qb, kb, vb, vt, ctx, gathered, wb,
    own_sem, qkv_send, qkv_recv, halo_send, halo_recv, ctx_send, ctx_recv,
    w1_send, w1_recv, w2_send, w2_recv, w3_send, w3_recv,
):
    blk = lax.axis_index("blk")
    zed = lax.axis_index("head")
    rows, d_model = q_in.shape
    w_rows = w_in.shape[0]
    pairs, span, _ = qb.shape
    width = pairs * PAIR
    cols = n_blk // 2
    column, core = blk // 2, blk % 2
    piece = d_model // n_blk
    half = d_model // 2
    others = range(1, n_head)

    def ds(start, size, unit):
        return pl.ds(pl.multiple_of(start, unit), size)

    def remote(src, dst, send, recv, device):
        return pltpu.make_async_remote_copy(
            src_ref=src, dst_ref=dst, send_sem=send, recv_sem=recv,
            device_id=device, device_id_type=MESH,
        )

    def to_head(d):
        return lax.rem(zed + d, n_head)

    def from_head(d):
        return lax.rem(zed + n_head - d, n_head)

    streams = ((k_in, kb, span), (v_in, vb, span), (q_in, qb, 0))

    def lands(a, g):
        _, buf, base = streams[a]
        return buf.at[g, ds(base + zed * rows, rows, 128)]

    def exchange(a, g, d):
        src = streams[a][0].at[:, ds(to_head(d) * width + g * PAIR, PAIR, 128)]
        return remote(
            src, lands(a, g), qkv_send.at[a, g, d - 1], qkv_recv.at[a, g, d - 1],
            (blk, to_head(d)),
        )

    def own(a, g):
        src = streams[a][0].at[:, ds(zed * width + g * PAIR, PAIR, 128)]
        return pltpu.make_async_copy(src, lands(a, g), own_sem.at[a, g])

    def halo(a, g):
        buf = streams[a][1]
        return remote(
            buf.at[g, pl.ds(span, span)], buf.at[g, pl.ds(0, span)],
            halo_send.at[a, g], halo_recv.at[a, g],
            (lax.rem(blk + 1, n_blk), zed),
        )

    def give_back(g, d):
        return remote(
            ctx.at[g, ds(to_head(d) * rows, rows, 128)],
            gathered.at[zed, :, pl.ds(g * PAIR, PAIR)],
            ctx_send.at[g, d - 1], ctx_recv.at[g, d - 1],
            (blk, to_head(d)),
        )

    my_piece = ds(core * half + column * piece, piece, 128)

    def w_along_head(d):
        return remote(
            w_in.at[:, my_piece], wb.at[ds(zed * w_rows, w_rows, 128), my_piece],
            w1_send.at[d - 1], w1_recv.at[d - 1], (blk, to_head(d)),
        )

    def w_in_plane(d, e):
        part = wb.at[ds(from_head(d) * w_rows, w_rows, 128), my_piece]
        return remote(
            part, part, w2_send.at[d - 1, e - 1], w2_recv.at[d - 1, e - 1],
            (lax.rem(blk + 2 * e, n_blk), zed),
        )

    def w_to_sibling(d):
        part = wb.at[
            ds(from_head(d) * w_rows, w_rows, 128), ds(core * half, half, 128)
        ]
        return remote(
            part, part, w3_send.at[d - 1], w3_recv.at[d - 1],
            (blk + 1 - 2 * core, zed),
        )

    w_own = pltpu.make_async_copy(
        w_in, wb.at[ds(zed * w_rows, w_rows, 128)], own_sem.at[3, 0]
    )

    for g in range(pairs):
        for a in range(3):
            own(a, g).start()
    w_own.start()

    barrier = pltpu.get_barrier_semaphore()
    peers = [(blk, to_head(d)) for d in others]
    peers += [(lax.rem(blk + 2 * e, n_blk), zed) for e in range(1, cols)]
    peers += [(lax.rem(blk + 1, n_blk), zed), (lax.rem(blk + n_blk - 1, n_blk), zed)]
    for peer in peers:
        pl.semaphore_signal(barrier, inc=1, device_id=peer, device_id_type=MESH)
    pl.semaphore_wait(barrier, len(peers))

    for g in range(pairs):
        for a in range(3):
            for d in others:
                exchange(a, g, d).start()
        if g == 0:
            for d in others:
                w_along_head(d).start()

    def arrived(a, g):
        own(a, g).wait()
        for d in others:
            exchange(a, g, d).wait_recv()

    def tile(g, c):
        row0 = c * rows
        query = qb[g, ds(row0, rows, 128), :].astype(jnp.float32)
        lane = lax.broadcasted_iota(jnp.int32, (rows, PAIR), 1)
        both = jnp.concatenate(
            [jnp.where(lane < HEAD_DIM, query, 0.0), jnp.where(lane < HEAD_DIM, 0.0, query)], 0
        ).astype(jnp.bfloat16)
        contract = (((1,), (1,)), ((), ()))
        far = lax.dot_general(
            kb[g, ds(row0, span, 128), :], both, contract, preferred_element_type=jnp.float32
        )
        near = lax.dot_general(
            kb[g, ds(row0 + span, rows, 128), :], both, contract,
            preferred_element_type=jnp.float32,
        )
        low = low_ref[c] - (blk * span - span + row0)
        low = jnp.concatenate([low, low], 1)
        key_far = lax.broadcasted_iota(jnp.int32, (span, 2 * rows), 0)
        key_near = lax.broadcasted_iota(jnp.int32, (rows, 2 * rows), 0)
        bin_near = lax.broadcasted_iota(jnp.int32, (rows, 2 * rows), 1)
        bin_near = jnp.where(bin_near >= rows, bin_near - rows, bin_near)
        far = jnp.where(key_far >= low, far * SCALE, -jnp.inf)
        near = jnp.where(
            (key_near >= low - span) & (key_near <= bin_near), near * SCALE, -jnp.inf
        )
        largest = jnp.maximum(
            jnp.max(far, axis=0, keepdims=True), jnp.max(near, axis=0, keepdims=True)
        )
        far = jnp.exp2(far - largest)
        near = jnp.exp2(near - largest)
        totals = jnp.sum(far, axis=0, keepdims=True) + jnp.sum(near, axis=0, keepdims=True)
        mixed = jnp.dot(
            vt[:, ds(row0, span, 128)], far.astype(jnp.bfloat16),
            preferred_element_type=jnp.float32,
        ) + jnp.dot(
            vt[:, ds(row0 + span, rows, 128)], near.astype(jnp.bfloat16),
            preferred_element_type=jnp.float32,
        )
        mixed = mixed / totals
        mixed = jnp.concatenate([mixed[:HEAD_DIM, :rows], mixed[HEAD_DIM:, rows:]], 0)
        return mixed.T.astype(jnp.bfloat16)

    def attend(g):
        halo(0, g).wait_recv()
        halo(1, g).wait_recv()
        vt[...] = vb[g].T

        def step(t, carry):
            chunks = [lax.rem(zed + 1 + 2 * t + u, n_head) for u in range(2)]
            tiles = [tile(g, c) for c in chunks]
            for u in range(2):
                ctx[g, ds(chunks[u] * rows, rows, 128), :] = tiles[u]
            for u in range(2):
                d = 2 * t + u + 1

                @pl.when(d < n_head)
                def _():
                    give_back(g, d).start()

            return carry

        lax.fori_loop(0, n_head // 2, step, 0)
        gathered[zed, :, pl.ds(g * PAIR, PAIR)] = ctx[g, ds(zed * rows, rows, 128), :]

    for g in range(pairs):
        arrived(0, g)
        arrived(1, g)
        halo(0, g).start()
        halo(1, g).start()
        arrived(2, g)
        if g == min(1, pairs - 1):
            for d in others:
                w_along_head(d).wait_recv()
                for e in range(1, cols):
                    w_in_plane(d, e).start()
        if g >= 1:
            attend(g - 1)
    for d in others:
        for e in range(1, cols):
            w_in_plane(d, e).wait_recv()
        w_to_sibling(d).start()
    attend(pairs - 1)
    w_own.wait()
    for d in others:
        w_to_sibling(d).wait_recv()
    for g in range(pairs):
        for d in others:
            give_back(g, d).wait_recv()

    tile_n = 512
    for n in range(d_model // tile_n):
        col = pl.ds(n * tile_n, tile_n)
        total = jnp.zeros((rows, tile_n), jnp.float32)
        for s in range(n_head):
            total += jnp.dot(
                gathered[s], wb[pl.ds(s * w_rows, w_rows), col],
                preferred_element_type=jnp.float32,
            )
        out_ref[:, col] = total.astype(out_ref.dtype)

    for g in range(pairs):
        for a in range(3):
            for d in others:
                exchange(a, g, d).wait_send()
        halo(0, g).wait_send()
        halo(1, g).wait_send()
        for d in others:
            give_back(g, d).wait_send()
    for d in others:
        w_along_head(d).wait_send()
        for e in range(1, cols):
            w_in_plane(d, e).wait_send()
        w_to_sibling(d).wait_send()


def on_device(n_blk, n_head, queries, key_rows, value_rows, w_out, first_key):
    rows, d_model = queries.shape
    span = rows * n_head
    width = d_model // n_head
    pairs = width // PAIR
    cols = n_blk // 2
    low = first_key.reshape(n_head, 1, rows)
    bf16 = jnp.bfloat16
    dma = pltpu.SemaphoreType.DMA
    hbm = pl.BlockSpec(memory_space=pl.ANY)
    vmem = pl.BlockSpec(memory_space=pltpu.VMEM)
    return pl.pallas_call(
        functools.partial(kernel, n_blk, n_head),
        out_shape=jax.ShapeDtypeStruct((rows, d_model), bf16),
        in_specs=[hbm, hbm, hbm, hbm, vmem],
        out_specs=vmem,
        scratch_shapes=[
            pltpu.VMEM((pairs, span, PAIR), bf16),
            pltpu.VMEM((pairs, 2 * span, PAIR), bf16),
            pltpu.VMEM((pairs, 2 * span, PAIR), bf16),
            pltpu.VMEM((PAIR, 2 * span), bf16),
            pltpu.VMEM((pairs, span, PAIR), bf16),
            pltpu.VMEM((n_head, rows, width), bf16),
            pltpu.VMEM((d_model, d_model), bf16),
            dma((4, pairs)),
            dma((3, pairs, n_head - 1)), dma((3, pairs, n_head - 1)),
            dma((2, pairs)), dma((2, pairs)),
            dma((pairs, n_head - 1)), dma((pairs, n_head - 1)),
            dma((n_head - 1,)), dma((n_head - 1,)),
            dma((n_head - 1, cols - 1)), dma((n_head - 1, cols - 1)),
            dma((n_head - 1,)), dma((n_head - 1,)),
        ],
        compiler_params=pltpu.CompilerParams(
            collective_id=0, has_side_effects=True, vmem_limit_bytes=48 * 1024 * 1024
        ),
    )(queries, key_rows, value_rows, w_out, low)


def solution(mesh):
    placed = (
        P(("blk", "head"), None),
        P(("blk", "head"), None),
        P(("blk", "head"), None),
        P("head", None),
        P("blk"),
    )
    body = functools.partial(on_device, mesh.shape["blk"], mesh.shape["head"])
    return jax.shard_map(
        body, mesh=mesh, in_specs=placed, out_specs=P(("blk", "head"), None), check_vma=False
    )
```

time: 212 us -> 112 us (0.53)
  Pallas kernels: 0 us -> 105 us
  blocking collectives: 68.9 us -> 0 us
  waiting for transfers between devices: 56.4 us -> 0 us
  matrix products: 28.8 us -> 0 us
  loops' own time: 18 us -> 0 us
  between operations: 13.5 us -> 0.01 us
  starting transfers between devices: 11.8 us -> 0 us
  other arithmetic: 4.42 us -> 0 us
  local copies, waits for them, and re-layouts: 8.85 us -> 6.19 us
    pallas_call x0 -> x1, Pallas kernels: none -> 105 us  [on_device(): pl.pallas_call(functools.partial(kernel, n_blk, n_head), out_shape=jax.Sh...]
    all_to_all x2 -> x0, blocking collectives: 68.9 us -> none  [the longest x1 39.2 us: on_device(): lax.all_to_all(value_rows, 'head', split_axis=1, concat_axis=0, tiled=True)]
    all_to_all x2 -> x0, waiting for transfers between devices: 49.6 us -> none  [the longest x1 26.6 us: on_device(): lax.all_to_all(queries, 'head', split_axis=1, concat_axis=0, tiled=True)]
    dot_general x17 -> x0, matrix products: 28.8 us -> none  [the longest x8 13.2 us: attend(): lax.dot_general(query_tile, key_tile, (((1,), (1,)), ((), ())), preferred...]
    another operation x1 -> x0, loops' own time: 18 us -> none  [on_device(): tiles = lax.map(one_tile, jnp.arange(spans * local_heads, dtype=jnp.int32))]
    all_to_all x2 -> x0, starting transfers between devices: 10.5 us -> none  [the longest x1 6.32 us: on_device(): lax.all_to_all(key_rows, 'head', split_axis=1, concat_axis=0, tiled=True)]
    all_gather x1 -> x0, waiting for transfers between devices: 6.14 us -> none  [on_device(): lax.all_gather(w_out, 'head', axis=0, tiled=True)]
    unnamed x6 -> x11, local copies, waits for them, and re-layouts: 0.33 us -> 6.19 us
  transfers between devices with their start and end apart: 4 -> 0, of which waited for: 3 -> 0; matrix products, arithmetic and copies ran while one was open for 17% -> 0% of each run, Pallas kernels for 0% -> 0%
where the time goes in v1:
time: 112 us
  Pallas kernels  105 us (94%)
  local copies, waits for them, and re-layouts  6.19 us (6%)
    pallas_call x1, Pallas kernels, on_device(): pl.pallas_call(functools.partial(kernel, n_blk, n_head), out_shape=jax.Sh...  105 us
    unnamed x11, local copies, waits for them, and re-layouts  6.19 us

profile of v1, /device:TPU:0, one launch (start us, length us, event | category | flops | bytes accessed | tf_op | source)
XLA Modules:
  0.0 111.7 jit_solution(16190664633001736900)
XLA Ops:
  0.0 0.0 copy-start
  0.0 1.6 %copy-done = bf16[512,2048]{1,0:T(8,128)(2,1)S(1)} copy-done((bf16[512,2048]{1,0:T(8,128)(2,1)S(1)}, bf16[512,2048]{1,0:T(8,128)(2,1)}, u32[]{:S(2)}) %copy-start) | copy-done | bytes 2097176
  1.6 0.0 copy-start.1
  1.6 1.0 copy-done.1
  2.6 0.0 copy-start.2
  2.6 1.0 copy-done.2
  3.7 0.0 copy-start.3
  3.7 1.0 copy-done.3
  4.7 0.0 copy-start.4
  4.7 0.7 copy-done.4
  5.4 105.5 %shard_map.55 = bf16[128,2048]{1,0:T(8,128)(2,1)S(1)} custom-call(bf16[128,2048]{1,0:T(8,128)(2,1)S(1)} %copy-done.1, bf16[128,2048]{1,0:T(8,128)(2,1)S(1)} %copy-done.2, bf16[128,2048]{1,0:T(8,128)(2,1)S(1)} %copy-done.3, bf16[512,2048]{1,0:T(8,128)(2,1)S(1)} %copy-done, s32[4,1,128]{2,1,0:T(1,128)S(1)} %bitcast.1), custom_call_target="tpu_custom_call" | custom-call | tf_op jit(solution)/shard_map/pallas_call | solution.py:263
  110.9 0.8 copy.7
Async XLA Ops:
  0.0 1.6 %copy-start = (bf16[512,2048]{1,0:T(8,128)(2,1)S(1)}, bf16[512,2048]{1,0:T(8,128)(2,1)}, u32[]{:S(2)}) copy-start(bf16[512,2048]{1,0:T(8,128)(2,1)} %w_in.1) | copy-start | bytes 6291460
  1.6 1.0 copy-start.1
  2.6 1.0 copy-start.2
  3.7 1.0 copy-start.3
  4.7 0.7 copy-start.4

commit v2 on v1

--- a/solution.py
+++ b/solution.py
@@ -16,7 +16,7 @@
 
 def kernel(
     n_blk, n_head, q_in, k_in, v_in, w_in, low_ref, out_ref,
-    qb, kb, vb, vt, ctx, gathered, wb,
+    qb, kb, vb, vt, ctx, gathered, wb, acc,
     own_sem, qkv_send, qkv_recv, halo_send, halo_recv, ctx_send, ctx_recv,
     w1_send, w1_recv, w2_send, w2_recv, w3_send, w3_recv,
 ):
@@ -82,27 +82,63 @@
 
     my_piece = ds(core * half + column * piece, piece, 128)
 
-    def w_along_head(d):
-        return remote(
-            w_in.at[:, my_piece], wb.at[ds(zed * w_rows, w_rows, 128), my_piece],
-            w1_send.at[d - 1], w1_recv.at[d - 1], (blk, to_head(d)),
-        )
-
-    def w_in_plane(d, e):
-        part = wb.at[ds(from_head(d) * w_rows, w_rows, 128), my_piece]
-        return remote(
-            part, part, w2_send.at[d - 1, e - 1], w2_recv.at[d - 1, e - 1],
+    def shard(s):
+        return ds(s * w_rows, w_rows, 128)
+
+    def w_hop(t, way):
+        s = zed - way * (t - 1)
+        part = wb.at[shard(s), my_piece]
+        at = (max(0, -way), t - 1)
+        return remote(
+            w_in.at[:, my_piece] if t == 1 else part, part,
+            w1_send.at[at], w1_recv.at[at], (blk, zed + way),
+        )
+
+    def hop_is_sent(t, way):
+        s, to = zed - way * (t - 1), zed + way
+        return (s >= 0) & (s < n_head) & (to >= 0) & (to < n_head)
+
+    def hop_arrives(t, way):
+        s = zed - way * t
+        return (s >= 0) & (s < n_head)
+
+    def w_got(t, way):
+        s = zed - way * t
+        part = wb.at[shard(s), my_piece]
+        at = (max(0, -way), t - 1)
+        return remote(part, part, w1_send.at[at], w1_recv.at[at], (blk, zed - way))
+
+    def w_in_plane(s, e):
+        part = wb.at[shard(s), my_piece]
+        return remote(
+            part, part, w2_send.at[s, e - 1], w2_recv.at[s, e - 1],
             (lax.rem(blk + 2 * e, n_blk), zed),
         )
 
-    def w_to_sibling(d):
-        part = wb.at[
-            ds(from_head(d) * w_rows, w_rows, 128), ds(core * half, half, 128)
-        ]
-        return remote(
-            part, part, w3_send.at[d - 1], w3_recv.at[d - 1],
-            (blk + 1 - 2 * core, zed),
-        )
+    def w_to_sibling(s):
+        part = wb.at[shard(s), ds(core * half, half, 128)]
+        return remote(
+            part, part, w3_send.at[s], w3_recv.at[s], (blk + 1 - 2 * core, zed),
+        )
+
+    def start_hop(t):
+        for way in (1, -1):
+            @pl.when(hop_is_sent(t, way))
+            def _():
+                w_hop(t, way).start()
+
+    def take_hop(t):
+        for way in (1, -1):
+            @pl.when(hop_arrives(t, way))
+            def _():
+                w_got(t, way).wait_recv()
+        if t < n_head - 1:
+            start_hop(t + 1)
+        for way in (1, -1):
+            @pl.when(hop_arrives(t, way))
+            def _():
+                for e in range(1, cols):
+                    w_in_plane(zed - way * t, e).start()
 
     w_own = pltpu.make_async_copy(
         w_in, wb.at[ds(zed * w_rows, w_rows, 128)], own_sem.at[3, 0]
@@ -121,13 +157,16 @@
         pl.semaphore_signal(barrier, inc=1, device_id=peer, device_id_type=MESH)
     pl.semaphore_wait(barrier, len(peers))
 
-    for g in range(pairs):
+    def send_pair(g):
         for a in range(3):
             for d in others:
                 exchange(a, g, d).start()
-        if g == 0:
-            for d in others:
-                w_along_head(d).start()
+
+    start_hop(1)
+    for t in range(1, n_head):
+        take_hop(t)
+    for g in range(pairs):
+        send_pair(g)
 
     def arrived(a, g):
         own(a, g).wait()
@@ -204,35 +243,41 @@
         halo(0, g).start()
         halo(1, g).start()
         arrived(2, g)
-        if g == min(1, pairs - 1):
-            for d in others:
-                w_along_head(d).wait_recv()
-                for e in range(1, cols):
-                    w_in_plane(d, e).start()
         if g >= 1:
             attend(g - 1)
     for d in others:
         for e in range(1, cols):
-            w_in_plane(d, e).wait_recv()
-        w_to_sibling(d).start()
+            w_in_plane(from_head(d), e).wait_recv()
+        w_to_sibling(from_head(d)).start()
     attend(pairs - 1)
     w_own.wait()
     for d in others:
-        w_to_sibling(d).wait_recv()
-    for g in range(pairs):
+        w_to_sibling(from_head(d)).wait_recv()
+    tile_n = 512
+
+    def project(first, last):
+        for n in range(d_model // tile_n):
+            col = pl.ds(n * tile_n, tile_n)
+            total = jnp.zeros((rows, tile_n), jnp.float32) if first == 0 else acc[:, col]
+            for s in range(n_head):
+                total += jnp.dot(
+                    gathered[s, :, first * PAIR:last * PAIR],
+                    wb[s * w_rows + first * PAIR:s * w_rows + last * PAIR, col],
+                    preferred_element_type=jnp.float32,
+                )
+            if last == pairs:
+                out_ref[:, col] = total.astype(out_ref.dtype)
+            else:
+                acc[:, col] = total
+
+    for g in range(pairs - 1):
         for d in others:
             give_back(g, d).wait_recv()
-
-    tile_n = 512
-    for n in range(d_model // tile_n):
-        col = pl.ds(n * tile_n, tile_n)
-        total = jnp.zeros((rows, tile_n), jnp.float32)
-        for s in range(n_head):
-            total += jnp.dot(
-                gathered[s], wb[pl.ds(s * w_rows, w_rows), col],
-                preferred_element_type=jnp.float32,
-            )
-        out_ref[:, col] = total.astype(out_ref.dtype)
+    if pairs > 1:
+        project(0, pairs - 1)
+    for d in others:
+        give_back(pairs - 1, d).wait_recv()
+    project(pairs - 1, pairs)
 
     for g in range(pairs):
         for a in range(3):
@@ -243,10 +288,13 @@
         for d in others:
             give_back(g, d).wait_send()
     for d in others:
-        w_along_head(d).wait_send()
+        for way in (1, -1):
+            @pl.when(hop_is_sent(d, way))
+            def _():
+                w_hop(d, way).wait_send()
         for e in range(1, cols):
-            w_in_plane(d, e).wait_send()
-        w_to_sibling(d).wait_send()
+            w_in_plane(from_head(d), e).wait_send()
+        w_to_sibling(from_head(d)).wait_send()
 
 
 def on_device(n_blk, n_head, queries, key_rows, value_rows, w_out, first_key):
@@ -273,16 +321,17 @@
             pltpu.VMEM((pairs, span, PAIR), bf16),
             pltpu.VMEM((n_head, rows, width), bf16),
             pltpu.VMEM((d_model, d_model), bf16),
+            pltpu.VMEM((rows, d_model), jnp.float32),
             dma((4, pairs)),
             dma((3, pairs, n_head - 1)), dma((3, pairs, n_head - 1)),
             dma((2, pairs)), dma((2, pairs)),
             dma((pairs, n_head - 1)), dma((pairs, n_head - 1)),
-            dma((n_head - 1,)), dma((n_head - 1,)),
-            dma((n_head - 1, cols - 1)), dma((n_head - 1, cols - 1)),
-            dma((n_head - 1,)), dma((n_head - 1,)),
+            dma((2, n_head - 1)), dma((2, n_head - 1)),
+            dma((n_head, cols - 1)), dma((n_head, cols - 1)),
+            dma((n_head,)), dma((n_head,)),
         ],
         compiler_params=pltpu.CompilerParams(
-            collective_id=0, has_side_effects=True, vmem_limit_bytes=48 * 1024 * 1024
+            collective_id=0, has_side_effects=True, vmem_limit_bytes=63 * 1024 * 1024
         ),
     )(queries, key_rows, value_rows, w_out, low)
 

time: 112 us -> 74.8 us (0.67)
  the two profiles are of different devices: /device:TPU:0 before, /device:TPU:29 now
where the time goes in v2:
time: 74.8 us; the launch traced here: 74.6 us
  Pallas kernels  72.8 us (97%)
  local copies, waits for them, and re-layouts  1.88 us (3%)
    pallas_call x1, Pallas kernels, on_device(): pl.pallas_call(functools.partial(kernel, n_blk, n_head), out_shape=jax.Sh...  72.8 us
    unnamed x1, local copies, waits for them, and re-layouts  1.88 us

profile of v2, /device:TPU:29, one launch (start us, length us, event | category | flops | bytes accessed | tf_op | source)
XLA Modules:
  0.0 74.6 jit_solution(3193333559080858721)
XLA Ops:
  0.0 72.8 %shard_map.55 = bf16[128,2048]{1,0:T(8,128)(2,1)} custom-call(bf16[128,2048]{1,0:T(8,128)(2,1)} %q_in.1, bf16[128,2048]{1,0:T(8,128)(2,1)} %k_in.1, bf16[128,2048]{1,0:T(8,128)(2,1)} %v_in.1, bf16[512,2048]{1,0:T(8,128)(2,1)} %w_in.1, s32[4,1,128]{2,1,0:T(1,128)} %bitcast.1), custom_call_target="tpu_custom_call" | custom-call | tf_op jit(solution)/shard_map/pallas_call | solution.py:311
  72.8 1.9 %copy.7 = bf16[128,2048]{1,0:T(8,128)(2,1)} copy(bf16[128,2048]{1,0:T(8,128)(2,1)} %shard_map.55) | data formatting | bytes 1048576

commit v3 on v2

--- a/solution.py
+++ b/solution.py
@@ -157,16 +157,20 @@
         pl.semaphore_signal(barrier, inc=1, device_id=peer, device_id_type=MESH)
     pl.semaphore_wait(barrier, len(peers))
 
-    def send_pair(g):
-        for a in range(3):
-            for d in others:
+    def send(arrays, g):
+        for a in arrays:
+            for d in sorted(others, key=lambda d: abs(d - n_head // 2)):
                 exchange(a, g, d).start()
 
     start_hop(1)
     for t in range(1, n_head):
+        if t == n_head - 1:
+            send((0, 1), 0)
         take_hop(t)
-    for g in range(pairs):
-        send_pair(g)
+    for g in range(1, pairs):
+        send((0, 1), g)
+        send((2,), g - 1)
+    send((2,), pairs - 1)
 
     def arrived(a, g):
         own(a, g).wait()
@@ -242,13 +246,14 @@
         arrived(1, g)
         halo(0, g).start()
         halo(1, g).start()
-        arrived(2, g)
         if g >= 1:
+            arrived(2, g - 1)
             attend(g - 1)
     for d in others:
         for e in range(1, cols):
             w_in_plane(from_head(d), e).wait_recv()
         w_to_sibling(from_head(d)).start()
+    arrived(2, pairs - 1)
     attend(pairs - 1)
     w_own.wait()
     for d in others:

time: 74.8 us -> 71 us (0.949)
  the two profiles are of different devices: /device:TPU:29 before, /device:TPU:0 now
where the time goes in v3:
time: 71 us; the launch traced here: 70.5 us
  Pallas kernels  68.6 us (97%)
  local copies, waits for them, and re-layouts  1.88 us (3%)
    pallas_call x1, Pallas kernels, on_device(): pl.pallas_call(functools.partial(kernel, n_blk, n_head), out_shape=jax.Sh...  68.6 us
    unnamed x1, local copies, waits for them, and re-layouts  1.88 us

profile of v3, /device:TPU:0, one launch (start us, length us, event | category | flops | bytes accessed | tf_op | source)
XLA Modules:
  0.0 70.5 jit_solution(9485190849984569374)
XLA Ops:
  0.0 68.6 %shard_map.55 = bf16[128,2048]{1,0:T(8,128)(2,1)} custom-call(bf16[128,2048]{1,0:T(8,128)(2,1)} %q_in.1, bf16[128,2048]{1,0:T(8,128)(2,1)} %k_in.1, bf16[128,2048]{1,0:T(8,128)(2,1)} %v_in.1, bf16[512,2048]{1,0:T(8,128)(2,1)} %w_in.1, s32[4,1,128]{2,1,0:T(1,128)} %bitcast.1), custom_call_target="tpu_custom_call" | custom-call | tf_op jit(solution)/shard_map/pallas_call | solution.py:316
  68.7 1.9 %copy.7 = bf16[128,2048]{1,0:T(8,128)(2,1)} copy(bf16[128,2048]{1,0:T(8,128)(2,1)} %shard_map.55) | data formatting | bytes 1048576

commit v4 on v3

--- a/solution.py
+++ b/solution.py
@@ -164,8 +164,10 @@
 
     start_hop(1)
     for t in range(1, n_head):
+        if t == max(1, n_head - 2):
+            send((0,), 0)
         if t == n_head - 1:
-            send((0, 1), 0)
+            send((1,), 0)
         take_hop(t)
     for g in range(1, pairs):
         send((0, 1), g)

time: 71 us -> 71 us (level)
  no operation moved by 1% of the time
where the time goes in v4:
time: 71 us; the launch traced here: 70.5 us
  Pallas kernels  68.6 us (97%)
  local copies, waits for them, and re-layouts  1.88 us (3%)
    pallas_call x1, Pallas kernels, on_device(): pl.pallas_call(functools.partial(kernel, n_blk, n_head), out_shape=jax.Sh...  68.6 us
    unnamed x1, local copies, waits for them, and re-layouts  1.88 us

profile of v4, /device:TPU:0, one launch (start us, length us, event | category | flops | bytes accessed | tf_op | source)
XLA Modules:
  0.0 70.5 jit_solution(7568128918757425857)
XLA Ops:
  0.0 68.6 %shard_map.55 = bf16[128,2048]{1,0:T(8,128)(2,1)} custom-call(bf16[128,2048]{1,0:T(8,128)(2,1)} %q_in.1, bf16[128,2048]{1,0:T(8,128)(2,1)} %k_in.1, bf16[128,2048]{1,0:T(8,128)(2,1)} %v_in.1, bf16[512,2048]{1,0:T(8,128)(2,1)} %w_in.1, s32[4,1,128]{2,1,0:T(1,128)} %bitcast.1), custom_call_target="tpu_custom_call" | custom-call | tf_op jit(solution)/shard_map/pallas_call | solution.py:318
  68.7 1.9 %copy.7 = bf16[128,2048]{1,0:T(8,128)(2,1)} copy(bf16[128,2048]{1,0:T(8,128)(2,1)} %shard_map.55) | data formatting | bytes 1048576
